TPU v7x, 512 devices: a whole 4x8x8 slice. The times are simulated.
512 devices in a mesh: dp: 16 (over y, core), seq: 32 (over x, z).
Axes of the slice: x: 4, y: 8, z: 8, core: 2. Of those that a mesh axis runs over, the one named last changes fastest.
Arguments:
- frame_in: bfloat16 [16, 4608, 1024], P('dp', 'seq'), may hold values from -120 to 120
- token_ids: int32 [16, 32, 60], P('dp', 'seq'), may hold values from 0 to 3327
- durations: int32 [16, 32, 60], P('dp', 'seq'), may hold values from 1 to 4, 144 in all within a row
- valid_len: int32 [16], P('dp'), may hold values from 1152 to 4608, as said below
- t_bin: int32 [16], P('dp'), may hold values from 0 to 63
- token_table: bfloat16 [3328, 512], P('seq'), may hold values from -6 to 6
- enc_weight: bfloat16 [512, 1024], replicated, may hold values from -0.25 to 0.25
- mod_table: float32 [64, 2048], replicated, may hold values from -1.2 to 2.5
- w_query: bfloat16 [1024, 512], P('seq'), may hold values from -0.1875 to 0.1875
- w_key: bfloat16 [1024, 512], P('seq'), may hold values from -0.1875 to 0.1875
- w_value: bfloat16 [1024, 512], P('seq'), may hold values from -0.1875 to 0.1875
- attn_grad: bfloat16 [16, 4608, 512], P('dp', 'seq'), may hold values from -6 to 6
Outputs:
- attn_out: bfloat16 [16, 4608, 512], P('dp', 'seq')
- frame_grad: bfloat16 [16, 4608, 1024], P('dp', 'seq')
- query_weight_grad: float32 [1024, 512], P('seq')
- key_weight_grad: float32 [1024, 512], P('seq')
- value_weight_grad: float32 [1024, 512], P('seq')
Inputs may be any that keep to these rules, and one draw needn't show every extreme that they name: In every slab the 60 durations sum to 144, so each token's frames lie in its own slab; some token lasts 4 frames. `valid_len`: some recording is valid over all 4608 frames.
All inputs are finite; a program needn't handle non-finite values.
Results may differ from a plain program's by a relative error of at most 0.017.
The roundings to bfloat16 on the way count: a program that leaves them out, or rounds other values in their place, can miss the bound.
Values may be sent and summed in bfloat16 or wider, within the bound.
A program may use at most 64 MiB of HBM per device.

v0:
```python
import math
import jax
import jax.numpy as jnp
from jax import lax
from jax.sharding import PartitionSpec as P

D = 1024
HEADS = 8
HD = 64
BLK = 48
QW = 512


def extended_2(cells, sides, width):
    for axis, dim in sides:
        count = lax.axis_size(axis)
        ends = count - 1
        head = lax.slice_in_dim(cells, 0, width, axis=dim)
        tail = lax.slice_in_dim(cells, cells.shape[dim] - width, cells.shape[dim], axis=dim)
        cells = jnp.concatenate(
            [
                lax.ppermute(tail, axis, [(i, (i + 1) % count) for i in range(ends)]),
                cells,
                lax.ppermute(head, axis, [((i + 1) % count, i) for i in range(ends)]),
            ],
            axis=dim,
        )
    return cells


def shifted(block, axis, distance):
    devices = range(lax.axis_size(axis))
    route = [(i - distance, i) for i in devices if i - distance in devices]
    return lax.ppermute(block, axis, route)


def attend_window(
    q_blocks, key_ext, value_ext, grad_out, query_pos, key_pos, valid_end, frames_total
):
    n_blocks = q_blocks.shape[0]
    block_len = q_blocks.shape[1]
    key_win = jnp.concatenate([key_ext[offset : offset + n_blocks] for offset in range(4)], axis=1)
    value_win = jnp.concatenate(
        [value_ext[offset : offset + n_blocks] for offset in range(4)], axis=1
    )
    key_here = key_pos[:, None, :]
    allowed = (
        (key_here >= 0)
        & (key_here < frames_total)
        & ((key_here < valid_end) | (query_pos[:, :, None] >= valid_end))
    )
    row_mask = allowed[:, None]
    inv_scale = 1.0 / math.sqrt(q_blocks.shape[-1])
    scores = (
        jnp.einsum("bqhd,bkhd->bhqk", q_blocks, key_win, preferred_element_type=jnp.float32)
        * inv_scale
    )
    scores = jnp.where(row_mask, scores, -1e30)
    row_top = jnp.max(scores, axis=-1, keepdims=True)
    shifted_exp = jnp.where(row_mask, jnp.exp(scores - row_top), 0.0)
    attn_prob = shifted_exp / jnp.sum(shifted_exp, axis=-1, keepdims=True)
    probs_low = attn_prob.astype(jnp.bfloat16)
    mixed_out = jnp.einsum(
        "bhqk,bkhd->bqhd", probs_low, value_win, preferred_element_type=jnp.float32
    ).astype(jnp.bfloat16)
    grad_probs = jnp.einsum(
        "bqhd,bkhd->bhqk", grad_out, value_win, preferred_element_type=jnp.float32
    )
    centre = jnp.sum(attn_prob * grad_probs, axis=-1, keepdims=True)
    grad_scores = (attn_prob * (grad_probs - centre) * inv_scale).astype(jnp.bfloat16)
    grad_query = jnp.einsum(
        "bhqk,bkhd->bqhd", grad_scores, key_win, preferred_element_type=jnp.float32
    ).astype(jnp.bfloat16)
    key_terms = jnp.einsum(
        "bhqk,bqhd->bkhd", grad_scores, q_blocks, preferred_element_type=jnp.float32
    )
    value_terms = jnp.einsum(
        "bhqk,bqhd->bkhd", probs_low, grad_out, preferred_element_type=jnp.float32
    )
    win_terms = jnp.concatenate([key_terms, value_terms], axis=2)
    pieces = win_terms.reshape(n_blocks, 4, block_len, win_terms.shape[2], win_terms.shape[3])
    folded = jnp.zeros((n_blocks + 3,) + pieces.shape[2:], jnp.float32)
    for offset in range(4):
        folded = folded + jnp.pad(pieces[:, offset], ((offset, 3 - offset), (0, 0), (0, 0), (0, 0)))
    return (mixed_out, grad_query, folded)


def pick_rows(wanted, table_piece):
    inside = (wanted >= 0) & (wanted < table_piece.shape[0])
    picked = jnp.take(table_piece, jnp.clip(wanted, 0, table_piece.shape[0] - 1), axis=0)
    return jnp.where(inside[:, None], picked, jnp.zeros_like(picked))


def shards(
    frame_in,
    token_ids,
    durations,
    valid_len,
    t_bin,
    token_table,
    enc_weight,
    mod_table,
    w_query,
    w_key,
    w_value,
    attn_grad,
):
    frames = frame_in[0]
    n_frames = frames.shape[0]
    seq_count = lax.axis_size("seq")
    seq_index = lax.axis_index("seq")
    dp_count = lax.axis_size("dp")
    frames_total = n_frames * seq_count
    valid_end = valid_len[0]
    wanted = token_ids[0, 0]
    token_emb = pick_rows(wanted, lax.all_gather(token_table, "seq", axis=0, tiled=True))
    token_ends = jnp.cumsum(durations[0, 0])
    local_pos = jnp.arange(n_frames, dtype=jnp.int32)
    owner_tok = jnp.sum((token_ends[None, :] <= local_pos[:, None]).astype(jnp.int32), axis=1)
    frame_emb = jnp.take(token_emb, owner_tok, axis=0)
    hidden_in = frames.astype(jnp.float32) + jnp.dot(
        frame_emb, enc_weight, preferred_element_type=jnp.float32
    )
    root_ms = jnp.sqrt(jnp.mean(hidden_in * hidden_in, axis=1, keepdims=True) + 1e-06)
    normed = hidden_in / root_ms
    modulation = lax.dynamic_index_in_dim(mod_table, t_bin[0], 0, keepdims=False)
    gain_part = 1.0 + modulation[:D]
    shift_part = modulation[D:]
    modulated = (normed * gain_part + shift_part).astype(jnp.bfloat16)
    shard_cat = jnp.concatenate([w_query, w_key, w_value], axis=1)
    weights_all = lax.all_gather(shard_cat, "seq", axis=0, tiled=True)
    projected = jnp.dot(modulated, weights_all, preferred_element_type=jnp.float32).astype(
        jnp.bfloat16
    )
    queries = projected[:, :QW]
    keys_values = projected[:, QW:]
    padded = extended_2(keys_values, (("seq", 0),), 2 * BLK)
    extended = padded[: n_frames + 3 * BLK]
    n_blocks = n_frames // BLK
    ext_blocks = extended.reshape(n_blocks + 3, BLK, 2, HEADS, HD)
    global_pos = seq_index * n_frames + local_pos
    query_pos = global_pos.reshape(n_blocks, BLK)
    key_pos = (
        seq_index * n_frames
        + (jnp.arange(n_blocks, dtype=jnp.int32)[:, None] - 2) * BLK
        + jnp.arange(4 * BLK, dtype=jnp.int32)[None, :]
    )
    live_rows = global_pos < valid_end
    grad_live = jnp.where(live_rows[:, None], attn_grad[0], jnp.zeros_like(attn_grad[0]))
    attn_blocks, query_grad, ext_grad = attend_window(
        queries.reshape(n_blocks, BLK, HEADS, HD),
        ext_blocks[:, :, 0],
        ext_blocks[:, :, 1],
        grad_live.reshape(n_blocks, BLK, HEADS, HD),
        query_pos,
        key_pos,
        valid_end,
        frames_total,
    )
    ext_rows = ext_grad.reshape(n_frames + 3 * BLK, 2 * QW)
    from_next = shifted(ext_rows[: 2 * BLK], "seq", -1)
    from_prev = shifted(ext_rows[n_frames + 2 * BLK :], "seq", 1)
    own_rows = ext_rows[2 * BLK : 2 * BLK + n_frames]
    own_rows = (
        own_rows
        + jnp.pad(from_next, ((n_frames - 2 * BLK, 0), (0, 0)))
        + jnp.pad(from_prev, ((0, n_frames - BLK), (0, 0)))
    )
    grad_cat = jnp.concatenate(
        [query_grad.reshape(n_frames, QW), own_rows.astype(jnp.bfloat16)], axis=1
    )
    grad_scale = 1.0 / math.sqrt(dp_count * frames_total)
    per_seq = lax.psum_scatter(
        (
            lax.dot_general(
                modulated, grad_cat, (((0,), (0,)), ((), ())), preferred_element_type=jnp.float32
            )
            * grad_scale
        ).astype(jnp.bfloat16),
        "seq",
        scatter_dimension=0,
        tiled=True,
    ).astype(jnp.float32)
    weight_grad = lax.psum(per_seq, "dp")
    hidden_grad = lax.dot_general(
        grad_cat, weights_all, (((1,), (1,)), ((), ())), preferred_element_type=jnp.float32
    )
    scaled_grad = hidden_grad * gain_part
    frame_grad = (
        scaled_grad - normed * jnp.mean(scaled_grad * normed, axis=1, keepdims=True)
    ) / root_ms
    return (
        attn_blocks.reshape(n_frames, QW)[None],
        frame_grad.astype(jnp.bfloat16)[None],
        weight_grad[:, :QW],
        weight_grad[:, QW : 2 * QW],
        weight_grad[:, 2 * QW :],
    )


def solution(mesh):
    placed = (
        P("dp", "seq", None),
        P("dp", "seq", None),
        P("dp", "seq", None),
        P("dp"),
        P("dp"),
        P("seq", None),
        P(),
        P(),
        P("seq", None),
        P("seq", None),
        P("seq", None),
        P("dp", "seq", None),
    )
    return jax.shard_map(
        shards,
        mesh=mesh,
        in_specs=placed,
        out_specs=(
            P("dp", "seq", None),
            P("dp", "seq", None),
            P("seq", None),
            P("seq", None),
            P("seq", None),
        ),
        check_vma=False,
    )
```

profile of v0, /device:TPU:25, one launch (start us, length us, event | category | flops | bytes accessed | tf_op | source)
XLA Modules:
  0.0 553.6 jit_solution(4595249403937196069)
XLA Ops:
  11.8 1.9 squeeze.30
  16.7 81.7 %all-gather.3.cloned.1.call-done = bf16[3328,512]{1,0:T(8,128)(2,1)} async-done(((bf16[104,512]{1,0:T(8,128)(2,1)}), bf16[3328,512]{1,0:T(8,128)(2,1)}) %all-gather.3.cloned.1.call-update) | async-done | bytes 3407888 | tf_op jit(solution)/shard_map/all_gather | solution.py:116
  98.5 3.1 gather_fusion
  103.1 81.1 %all-gather.5.cloned.1.call-done = bf16[1024,1536]{1,0:T(8,128)(2,1)} async-done(((bf16[32,1536]{1,0:T(8,128)(2,1)}), bf16[1024,1536]{1,0:T(8,128)(2,1)}) %all-gather.5.cloned.1.call-update) | async-done | bytes 3145744 | tf_op jit(solution)/shard_map/all_gather | solution.py:131
  184.2 2.6 convolution_convert_fusion
  186.8 2.8 collective-permute-start
  192.3 3.8 collective-permute-done.1
  199.6 2.1 copy.74
  206.2 3.3 fusion.56
  209.5 2.1 convolution_bitcast_fusion
  211.6 2.0 fusion.24
  213.6 10.4 %convolution_bitcast_fusion.1 = f32[3,192,8,64]{1,3,2,0:T(8,128)} fusion(f32[3,8,48,192]{3,2,1,0:T(8,128)} %fusion.24, bf16[3,48,8,64]{3,2,1,0:T(8,128)(2,1)} %reshape.221, f32[3,8,48,192]{3,2,1,0:T(8,128)} %get-tuple-element.29, f32[3,8,48]{2,1,0:T(8,128)S(1)} %get-tuple-element.28), kind=kOutput, calls=%fused_computation.10 | convolution fusion | flops 29861184 | bytes 3101184 | tf_op jit(solution)/shard_map/bhqk,bqhd->bkhd/dot_general | solution.py:74
  224.0 3.5 pad_maximum_fusion
  227.5 5.9 %copy.64 = f32[3,192,16,64]{3,2,1,0:T(8,128)} copy(f32[3,192,16,64]{1,3,2,0:T(8,128)} %pad_maximum_fusion) | data formatting | bytes 4718592 | tf_op jit(solution)/shard_map/concatenate | solution.py:80
  233.4 2.7 slice_bitcast_fusion.3
  240.0 2.2 slice.152
  244.6 1.8 slice.154
  246.4 4.5 collective-permute-start.3
  250.9 10.3 %fusion.11 = bf16[3,48,8,64]{3,1,2,0:T(8,128)(2,1)S(1)} fusion(f32[3,8,48,192]{3,2,1,0:T(8,128)} %fusion.24, bf16[3,48,8,64]{1,3,2,0:T(8,128)(2,1)} %bitcast.85, bf16[3,48,8,64]{1,3,2,0:T(8,128)(2,1)} %bitcast.80, bf16[3,48,8,64]{1,3,2,0:T(8,128)(2,1)} %bitcast.83, bf16[3,48,8,64]{1,3,2,0:T(8,128)(2,1)} %bitcast.79, ...), kind=kOutput, calls=%fused_computation.28 | convolution fusion | flops 32294208 | bytes 2511360 | tf_op jit(solution)/shard_map/bhqk,bkhd->bqhd/dot_general | solution.py:71
  263.8 2.7 multiply_convert_fusion
  267.9 2.2 fusion.10
  271.0 3.3 multiply_reduce_fusion.1
  275.2 218.2 %reduce-scatter.2.cloned.1.call-done = bf16[32,1536]{1,0:T(8,128)(2,1)} async-done(((bf16[1024,1536]{1,0:T(8,128)(2,1)}), bf16[32,1536]{1,0:T(8,128)(2,1)}) %reduce-scatter.2.cloned.1.call-update) | async-done | bytes 98320 | tf_op jit(solution)/shard_map/reduce_scatter | solution.py:173
  493.4 53.0 %all-reduce.7 = f32[32,1536]{1,0:T(8,128)S(1)} all-reduce(bf16[32,1536]{1,0:T(8,128)(2,1)} %reduce-scatter.2.cloned.1.call-done), channel_id=1, replica_groups=mesh['dp'=16,'seq'=32] {'dp'}, use_global_device_ids=true, to_apply=%region_8.9 | all-reduce | flops 49152 | bytes 294912 | tf_op jit(solution)/shard_map/psum | solution.py:184
  (130 shorter events, 31.1 us)
Async XLA Ops:
  7.2 95.4 %copy-start = (bf16[512,1024]{1,0:T(8,128)(2,1)S(1)}, bf16[512,1024]{1,0:T(8,128)(2,1)}, u32[]{:S(2)}) copy-start(bf16[512,1024]{1,0:T(8,128)(2,1)} %param.18) | copy-start | bytes 3145732
  7.2 91.3 %all-gather.3.cloned.1.call-start = ((), (), s32[]{:S(2)}) async-start(), calls=%async_computation.1 | async-start | bytes 3514368 | tf_op jit(solution)/shard_map/all_gather | solution.py:116
  7.9 176.3 %all-gather.5.cloned.1.call-start = ((), (), s32[]{:S(2)}) async-start(), calls=%async_computation.2 | async-start | bytes 3244032 | tf_op jit(solution)/shard_map/all_gather | solution.py:131
  9.4 484.0 %reduce-scatter.2.cloned.1.call-start = ((), (), s32[]{:S(2)}) async-start(), calls=%async_computation.3 | async-start | bytes 3244032 | tf_op jit(solution)/shard_map/reduce_scatter | solution.py:173
  11.7 90.8 %copy-start.22 = (bf16[1,144,1024]{2,1,0:T(8,128)(2,1)S(1)}, bf16[1,144,1024]{2,1,0:T(8,128)(2,1)}, u32[]{:S(2)}) copy-start(bf16[1,144,1024]{2,1,0:T(8,128)(2,1)} %param.12) | copy-start | bytes 884740
  15.3 168.9 %copy-start.24 = (f32[1,1024]{1,0:T(1,128)}, f32[1,1024]{1,0:T(1,128)S(1)}, u32[]{:S(2)}) copy-start(f32[1,1024]{1,0:T(1,128)S(1)} %get-tuple-element.17) | copy-start | bytes 12292
  15.3 168.9 %copy-start.27 = (f32[1,1024]{1,0:T(1,128)}, f32[1,1024]{1,0:T(1,128)S(1)}, u32[]{:S(2)}) copy-start(f32[1,1024]{1,0:T(1,128)S(1)} %get-tuple-element.18) | copy-start | bytes 12292
  103.1 83.7 %copy-start.6 = (f32[144,1024]{1,0:T(8,128)}, f32[144,1024]{1,0:T(8,128)S(1)}, u32[]{:S(2)}) copy-start(f32[144,1024]{1,0:T(8,128)S(1)} %get-tuple-element.27) | copy-start | bytes 1769476
  103.1 81.1 %copy-start.29 = (f32[144]{0:T(256)}, f32[144]{0:T(256)S(1)}, u32[]{:S(2)}) copy-start(f32[144]{0:T(256)S(1)} %add_sqrt_fusion) | copy-start | bytes 1732
  186.8 5.4 collective-permute-start
  189.7 6.4 %collective-permute-start.1 = (bf16[96,1024]{1,0:T(8,128)(2,1)S(1)}, bf16[96,1024]{1,0:T(8,128)(2,1)S(1)}, u32[]{:S(2)}, u32[]{:S(2)}) collective-permute-start(bf16[96,1024]{1,0:T(8,128)(2,1)S(1)} %get-tuple-element.20), channel_id=1, source_target_pairs={{1,0},{2,1},{3,2},{4,3},{5,4},{6,5},{7,6},{8,7},{9,8},{10,9},{11,1... | collective-permute-start | bytes 589832 | tf_op jit(solution)/shard_map/ppermute | solution.py:24
  198.3 3.3 copy-start.9
  198.3 4.3 copy-start.8
  199.6 6.6 %copy-start.18 = (bf16[3,48,1,8,64]{1,4,3,0,2:T(8,128)(2,1)}, bf16[3,48,1,8,64]{1,4,3,0,2:T(8,128)(2,1)S(1)}, u32[]{:S(2)}) copy-start(bf16[3,48,1,8,64]{1,4,3,0,2:T(8,128)(2,1)S(1)} %copy.72) | copy-start | bytes 442372
  204.9 6.7 %copy-start.14 = (bf16[3,48,1,8,64]{1,4,3,0,2:T(8,128)(2,1)}, bf16[3,48,1,8,64]{1,4,3,0,2:T(8,128)(2,1)S(1)}, u32[]{:S(2)}) copy-start(bf16[3,48,1,8,64]{1,4,3,0,2:T(8,128)(2,1)S(1)} %copy.69) | copy-start | bytes 442372
  206.2 3.3 copy-start.20
  209.5 4.1 copy-start.32
  242.1 19.7 %collective-permute-start.2 = (f32[96,1024]{1,0:T(8,128)}, f32[96,1024]{1,0:T(8,128)}, u32[]{:S(2)}, u32[]{:S(2)}) collective-permute-start(f32[96,1024]{1,0:T(8,128)} %slice.152), channel_id=1, source_target_pairs={{1,0},{2,1},{3,2},{4,3},{5,4},{6,5},{7,6},{8,7},{9,8},{10,9},{11,1... | collective-permute-start | bytes 1179656 | tf_op jit(solution)/shard_map/ppermute | solution.py:34
  243.8 7.1 %copy-start.33 = (f32[3,8,48]{2,1,0:T(8,128)S(1)}, f32[3,8,48]{2,1,0:T(8,128)}, u32[]{:S(2)}) copy-start(f32[3,8,48]{2,1,0:T(8,128)} %copy-done.32) | copy-start | bytes 13828
  246.4 15.5 %collective-permute-start.3 = (f32[48,1024]{1,0:T(8,128)}, f32[48,1024]{1,0:T(8,128)}, u32[]{:S(2)}, u32[]{:S(2)}) collective-permute-start(f32[48,1024]{1,0:T(8,128)} %slice.154), channel_id=1, source_target_pairs={{0,1},{1,2},{2,3},{3,4},{4,5},{5,6},{6,7},{7,8},{8,9},{9,10},{10,1... | collective-permute-start | bytes 589832 | tf_op jit(solution)/shard_map/ppermute | solution.py:34
  250.9 10.6 %slice-start = ((f32[6,48,16,64]{3,2,1,0:T(8,128)}), f32[3,48,16,64]{3,2,1,0:T(8,128)S(1)}, s32[]{:S(2)}) async-start(f32[6,48,16,64]{3,2,1,0:T(8,128)} %copy-done.5), calls=%async_computation.4 | async-start | bytes 2359296 | tf_op jit(solution)/shard_map/slice | solution.py:163
  261.4 2.3 copy-start.7
  267.9 3.2 copy-start.26
  267.9 3.2 copy-start.31
  (19 other events, 29.5 us)
Sparse Core Ops, SparseCore 0:
  11.2 87.2 all-gather.2
  102.2 81.9 all-gather.4
  266.7 226.6 reduce-scatter.1
where the time goes:
time: 555 us; the launch traced here: 554 us
  waiting for transfers between devices  386 us (70%)
  blocking collectives  53 us (10%)
  matrix products  39.3 us (7%)
  local copies, waits for them, and re-layouts  38.3 us (7%)
  between operations  15.5 us (3%)
  other arithmetic  11.6 us (2%)
  starting transfers between devices  10.3 us (2%)
    reduce_scatter x1, waiting for transfers between devices, shards(): lax.psum_scatter((lax.dot_general(modulated, grad_cat, (((0,), (0,)), (()...  218 us
    all_gather x1, waiting for transfers between devices, shards(): lax.all_gather(token_table, 'seq', axis=0, tiled=True)  81.7 us
    all_gather x1, waiting for transfers between devices, shards(): weights_all = lax.all_gather(shard_cat, 'seq', axis=0, tiled=True)  81.1 us
    psum x1, blocking collectives, shards(): weight_grad = lax.psum(per_seq, 'dp')  53 us
    unnamed x78, local copies, waits for them, and re-layouts  12.7 us
  transfers between devices with their start and end apart: 7, of which 4 were waited for; matrix products, arithmetic and copies ran while one was open for 6% of the time, Pallas kernels for 0%

commit v1 on v0

--- a/solution.py
+++ b/solution.py
@@ -181,7 +181,8 @@
         scatter_dimension=0,
         tiled=True,
     ).astype(jnp.float32)
-    weight_grad = lax.psum(per_seq, "dp")
+    shards_2 = lax.all_gather(per_seq, "dp")
+    weight_grad = jnp.sum(shards_2, axis=0)
     hidden_grad = lax.dot_general(
         grad_cat, weights_all, (((1,), (1,)), ((), ())), preferred_element_type=jnp.float32
     )

time: 555 us -> 554 us (level)
  the two profiles are of different devices: /device:TPU:25 before, /device:TPU:1 now
where the time goes in v1:
time: 554 us; the launch traced here: 553 us
  waiting for transfers between devices  435 us (79%)
  matrix products  39.3 us (7%)
  local copies, waits for them, and re-layouts  37.1 us (7%)
  between operations  15.6 us (3%)
  other arithmetic  15.2 us (3%)
  starting transfers between devices  10.4 us (2%)
    reduce_scatter x1, waiting for transfers between devices, shards(): lax.psum_scatter((lax.dot_general(modulated, grad_cat, (((0,), (0,)), (()...  227 us
    all_gather x1, waiting for transfers between devices, shards(): lax.all_gather(token_table, 'seq', axis=0, tiled=True)  82.8 us
    all_gather x1, waiting for transfers between devices, shards(): weights_all = lax.all_gather(shard_cat, 'seq', axis=0, tiled=True)  81.1 us
    all_gather x1, waiting for transfers between devices, shards(): shards_2 = lax.all_gather(per_seq, 'dp')  39.9 us
    unnamed x78, local copies, waits for them, and re-layouts  11.4 us
  transfers between devices with their start and end apart: 8, of which 5 were waited for; matrix products, arithmetic and copies ran while one was open for 6% of the time, Pallas kernels for 0%

profile of v1, /device:TPU:1, one launch (start us, length us, event | category | flops | bytes accessed | tf_op | source)
XLA Modules:
  0.0 552.9 jit_solution(12460795125888865189)
XLA Ops:
  11.8 1.9 squeeze.30
  16.7 82.8 %all-gather.5.cloned.1.call-done = bf16[3328,512]{1,0:T(8,128)(2,1)} async-done(((bf16[104,512]{1,0:T(8,128)(2,1)}), bf16[3328,512]{1,0:T(8,128)(2,1)}) %all-gather.5.cloned.1.call-update) | async-done | bytes 3407888 | tf_op jit(solution)/shard_map/all_gather | solution.py:116
  99.6 3.1 gather_fusion
  104.2 81.1 %all-gather.7.cloned.1.call-done = bf16[1024,1536]{1,0:T(8,128)(2,1)} async-done(((bf16[32,1536]{1,0:T(8,128)(2,1)}), bf16[1024,1536]{1,0:T(8,128)(2,1)}) %all-gather.7.cloned.1.call-update) | async-done | bytes 3145744 | tf_op jit(solution)/shard_map/all_gather | solution.py:131
  185.3 2.6 convolution_convert_fusion
  187.9 2.8 collective-permute-start
  193.4 3.8 collective-permute-done.1
  200.7 2.1 copy.74
  207.3 3.3 fusion.56
  210.6 2.1 convolution_bitcast_fusion
  212.8 2.0 fusion.24
  214.7 10.5 %convolution_bitcast_fusion.1 = f32[3,192,8,64]{1,3,2,0:T(8,128)} fusion(f32[3,8,48,192]{3,2,1,0:T(8,128)} %fusion.24, bf16[3,48,8,64]{3,2,1,0:T(8,128)(2,1)} %reshape.221, f32[3,8,48,192]{3,2,1,0:T(8,128)} %get-tuple-element.29, f32[3,8,48]{2,1,0:T(8,128)S(1)} %get-tuple-element.28), kind=kOutput, calls=%fused_computation.10 | convolution fusion | flops 29861184 | bytes 3101184 | tf_op jit(solution)/shard_map/bhqk,bqhd->bkhd/dot_general | solution.py:74
  225.2 3.5 pad_maximum_fusion
  228.7 5.9 %copy.64 = f32[3,192,16,64]{3,2,1,0:T(8,128)} copy(f32[3,192,16,64]{1,3,2,0:T(8,128)} %pad_maximum_fusion) | data formatting | bytes 4718592 | tf_op jit(solution)/shard_map/concatenate | solution.py:80
  234.6 2.7 slice_bitcast_fusion.3
  241.2 2.2 slice.152
  247.5 4.5 collective-permute-start.3
  252.0 10.3 %fusion.11 = bf16[3,48,8,64]{3,1,2,0:T(8,128)(2,1)S(1)} fusion(f32[3,8,48,192]{3,2,1,0:T(8,128)} %fusion.24, bf16[3,48,8,64]{1,3,2,0:T(8,128)(2,1)} %bitcast.87, bf16[3,48,8,64]{1,3,2,0:T(8,128)(2,1)} %bitcast.82, bf16[3,48,8,64]{1,3,2,0:T(8,128)(2,1)} %bitcast.85, bf16[3,48,8,64]{1,3,2,0:T(8,128)(2,1)} %bitcast.81, ...), kind=kOutput, calls=%fused_computation.28 | convolution fusion | flops 32294208 | bytes 2511360 | tf_op jit(solution)/shard_map/bhqk,bkhd->bqhd/dot_general | solution.py:71
  265.0 2.7 multiply_convert_fusion
  267.8 226.9 %reduce-scatter.2.cloned.1.call-done = bf16[32,1536]{1,0:T(8,128)(2,1)} async-done(((bf16[1024,1536]{1,0:T(8,128)(2,1)}), bf16[32,1536]{1,0:T(8,128)(2,1)}) %reduce-scatter.2.cloned.1.call-update) | async-done | bytes 98320 | tf_op jit(solution)/shard_map/reduce_scatter | solution.py:173
  496.4 2.2 fusion.10
  499.6 3.3 multiply_reduce_fusion.1
  503.8 39.9 %all-gather.9.cloned.1.call-done = f32[512,1536]{1,0:T(8,128)} async-done(((f32[32,1536]{1,0:T(8,128)}), f32[512,1536]{1,0:T(8,128)}) %all-gather.9.cloned.1.call-update) | async-done | bytes 3145744 | tf_op jit(solution)/shard_map/all_gather | solution.py:184
  543.7 2.1 reduce_sum.62
  (134 shorter events, 33.2 us)
Async XLA Ops:
  7.2 96.5 %copy-start = (bf16[512,1024]{1,0:T(8,128)(2,1)S(1)}, bf16[512,1024]{1,0:T(8,128)(2,1)}, u32[]{:S(2)}) copy-start(bf16[512,1024]{1,0:T(8,128)(2,1)} %param.18) | copy-start | bytes 3145732
  7.2 92.4 %all-gather.5.cloned.1.call-start = ((), (), s32[]{:S(2)}) async-start(), calls=%async_computation.1 | async-start | bytes 3514368 | tf_op jit(solution)/shard_map/all_gather | solution.py:116
  7.9 177.4 %all-gather.7.cloned.1.call-start = ((), (), s32[]{:S(2)}) async-start(), calls=%async_computation.2 | async-start | bytes 3244032 | tf_op jit(solution)/shard_map/all_gather | solution.py:131
  9.4 485.3 %reduce-scatter.2.cloned.1.call-start = ((), (), s32[]{:S(2)}) async-start(), calls=%async_computation.3 | async-start | bytes 3244032 | tf_op jit(solution)/shard_map/reduce_scatter | solution.py:173
  11.7 91.9 %copy-start.22 = (bf16[1,144,1024]{2,1,0:T(8,128)(2,1)S(1)}, bf16[1,144,1024]{2,1,0:T(8,128)(2,1)}, u32[]{:S(2)}) copy-start(bf16[1,144,1024]{2,1,0:T(8,128)(2,1)} %param.12) | copy-start | bytes 884740
  15.3 170.0 %copy-start.24 = (f32[1,1024]{1,0:T(1,128)}, f32[1,1024]{1,0:T(1,128)S(1)}, u32[]{:S(2)}) copy-start(f32[1,1024]{1,0:T(1,128)S(1)} %get-tuple-element.17) | copy-start | bytes 12292
  15.3 170.0 %copy-start.27 = (f32[1,1024]{1,0:T(1,128)}, f32[1,1024]{1,0:T(1,128)S(1)}, u32[]{:S(2)}) copy-start(f32[1,1024]{1,0:T(1,128)S(1)} %get-tuple-element.18) | copy-start | bytes 12292
  104.2 83.7 %copy-start.6 = (f32[144,1024]{1,0:T(8,128)}, f32[144,1024]{1,0:T(8,128)S(1)}, u32[]{:S(2)}) copy-start(f32[144,1024]{1,0:T(8,128)S(1)} %get-tuple-element.27) | copy-start | bytes 1769476
  104.2 81.1 %copy-start.29 = (f32[144]{0:T(256)}, f32[144]{0:T(256)S(1)}, u32[]{:S(2)}) copy-start(f32[144]{0:T(256)S(1)} %add_sqrt_fusion) | copy-start | bytes 1732
  187.9 5.4 collective-permute-start
  190.8 6.4 %collective-permute-start.1 = (bf16[96,1024]{1,0:T(8,128)(2,1)S(1)}, bf16[96,1024]{1,0:T(8,128)(2,1)S(1)}, u32[]{:S(2)}, u32[]{:S(2)}) collective-permute-start(bf16[96,1024]{1,0:T(8,128)(2,1)S(1)} %get-tuple-element.20), channel_id=1, source_target_pairs={{1,0},{2,1},{3,2},{4,3},{5,4},{6,5},{7,6},{8,7},{9,8},{10,9},{11,1... | collective-permute-start | bytes 589832 | tf_op jit(solution)/shard_map/ppermute | solution.py:24
  199.4 4.4 copy-start.8
  200.7 6.6 %copy-start.18 = (bf16[3,48,1,8,64]{1,4,3,0,2:T(8,128)(2,1)}, bf16[3,48,1,8,64]{1,4,3,0,2:T(8,128)(2,1)S(1)}, u32[]{:S(2)}) copy-start(bf16[3,48,1,8,64]{1,4,3,0,2:T(8,128)(2,1)S(1)} %copy.72) | copy-start | bytes 442372
  206.0 6.7 %copy-start.14 = (bf16[3,48,1,8,64]{1,4,3,0,2:T(8,128)(2,1)}, bf16[3,48,1,8,64]{1,4,3,0,2:T(8,128)(2,1)S(1)}, u32[]{:S(2)}) copy-start(bf16[3,48,1,8,64]{1,4,3,0,2:T(8,128)(2,1)S(1)} %copy.69) | copy-start | bytes 442372
  243.3 19.7 %collective-permute-start.2 = (f32[96,1024]{1,0:T(8,128)}, f32[96,1024]{1,0:T(8,128)}, u32[]{:S(2)}, u32[]{:S(2)}) collective-permute-start(f32[96,1024]{1,0:T(8,128)} %slice.152), channel_id=1, source_target_pairs={{1,0},{2,1},{3,2},{4,3},{5,4},{6,5},{7,6},{8,7},{9,8},{10,9},{11,1... | collective-permute-start | bytes 1179656 | tf_op jit(solution)/shard_map/ppermute | solution.py:34
  244.9 7.1 %copy-start.33 = (f32[3,8,48]{2,1,0:T(8,128)S(1)}, f32[3,8,48]{2,1,0:T(8,128)}, u32[]{:S(2)}) copy-start(f32[3,8,48]{2,1,0:T(8,128)} %copy-done.32) | copy-start | bytes 13828
  247.5 15.5 %collective-permute-start.3 = (f32[48,1024]{1,0:T(8,128)}, f32[48,1024]{1,0:T(8,128)}, u32[]{:S(2)}, u32[]{:S(2)}) collective-permute-start(f32[48,1024]{1,0:T(8,128)} %slice.154), channel_id=1, source_target_pairs={{0,1},{1,2},{2,3},{3,4},{4,5},{5,6},{6,7},{7,8},{8,9},{9,10},{10,1... | collective-permute-start | bytes 589832 | tf_op jit(solution)/shard_map/ppermute | solution.py:34
  252.0 10.6 %slice-start = ((f32[6,48,16,64]{3,2,1,0:T(8,128)}), f32[3,48,16,64]{3,2,1,0:T(8,128)S(1)}, s32[]{:S(2)}) async-start(f32[6,48,16,64]{3,2,1,0:T(8,128)} %copy-done.5), calls=%async_computation.5 | async-start | bytes 2359296 | tf_op jit(solution)/shard_map/slice | solution.py:163
  267.7 228.6 %copy-start.11 = (bf16[3,48,1,8,64]{1,4,3,0,2:T(8,128)(2,1)S(1)}, bf16[3,48,1,8,64]{1,4,3,0,2:T(8,128)(2,1)}, u32[]{:S(2)}) copy-start(bf16[3,48,1,8,64]{1,4,3,0,2:T(8,128)(2,1)} %copy.71) | copy-start | bytes 442372
  267.7 228.7 %copy-start.13 = (bf16[3,48,1,8,64]{1,4,3,0,2:T(8,128)(2,1)S(1)}, bf16[3,48,1,8,64]{1,4,3,0,2:T(8,128)(2,1)}, u32[]{:S(2)}) copy-start(bf16[3,48,1,8,64]{1,4,3,0,2:T(8,128)(2,1)} %copy.70) | copy-start | bytes 442372
  267.7 228.7 %copy-start.15 = (bf16[3,48,1,8,64]{1,4,3,0,2:T(8,128)(2,1)S(1)}, bf16[3,48,1,8,64]{1,4,3,0,2:T(8,128)(2,1)}, u32[]{:S(2)}) copy-start(bf16[3,48,1,8,64]{1,4,3,0,2:T(8,128)(2,1)} %copy-done.14) | copy-start | bytes 442372
  267.7 228.7 %copy-start.17 = (bf16[3,48,1,8,64]{1,4,3,0,2:T(8,128)(2,1)S(1)}, bf16[3,48,1,8,64]{1,4,3,0,2:T(8,128)(2,1)}, u32[]{:S(2)}) copy-start(bf16[3,48,1,8,64]{1,4,3,0,2:T(8,128)(2,1)} %copy.68) | copy-start | bytes 442372
  267.7 228.7 %copy-start.34 = (f32[3,8,48]{2,1,0:T(8,128)S(1)}, f32[3,8,48]{2,1,0:T(8,128)}, u32[]{:S(2)}) copy-start(f32[3,8,48]{2,1,0:T(8,128)} %copy-done.32) | copy-start | bytes 13828
  267.8 275.9 %all-gather.9.cloned.1.call-start = ((), (), s32[]{:S(2)}) async-start(), calls=%async_computation.4 | async-start | bytes 3342336 | tf_op jit(solution)/shard_map/all_gather | solution.py:184
  (20 other events, 42.9 us)
Sparse Core Ops, SparseCore 0:
  11.2 88.3 all-gather.4
  103.3 81.9 all-gather.6
  267.9 226.8 reduce-scatter.1
  496.9 46.6 all-gather.8
